TPU v7x, 32 devices: a whole 2x2x4 slice. The times are simulated.
32 devices in a mesh: group: 4 (over z), peer: 8 (over y, x, core).
Axes of the slice: x: 2, y: 2, z: 4, core: 2. Of those that a mesh axis runs over, the one named last changes fastest.
Arguments:
- embed: bfloat16 [16384, 1024], P(('group', 'peer')), may hold values from -64 to 64
- lengths: int32 [4, 512], P('group'), may hold values from 0 to 8, as said below
- w_in: bfloat16 [1024, 2048], replicated, may hold values from -0.1875 to 0.1875
- w_out: bfloat16 [512, 1024], replicated, may hold values from -0.25 to 0.25
- cotangent: bfloat16 [8192, 1024], P(('group', 'peer')), may hold values from -6 to 6
Outputs:
- out_work: bfloat16 [8192, 1024], P(('group', 'peer'))
- grad_home: bfloat16 [16384, 1024], P(('group', 'peer'))
- grad_out_proj: float32 [512, 1024], P('peer', 'group')
Inputs may be any that keep to these rules, and one draw needn't show every extreme that they name: `lengths`: in every group exactly 256 blocks are live, and some peer of every group has all 64 of its blocks live; some block of every group has length 8.
All inputs are finite; a program needn't handle non-finite values.
Results may differ from a plain program's by a relative error of at most 0.0087.
Values may be sent and summed in bfloat16 or wider, within the bound.
A program may use at most 64 MiB of HBM per device.

v0:
```python
import math

import jax
import jax.numpy as jnp
from jax import lax
from jax.sharding import PartitionSpec as P

HD = 128
BLK = 8


EPSILON = 1e-06
MIX_FLOOR = 1.0


def shortened(shard):

    def short(part):
        return part.astype(jnp.bfloat16) if part.dtype == jnp.float32 else part

    return jax.tree.map(short, shard)


def plan_tables(block_lengths):
    block_total = block_lengths.shape[1]
    is_live = (block_lengths > 0).astype(jnp.int32)
    counts = jnp.sum(is_live, axis=1)
    prefix = jnp.cumsum(counts) - counts
    block_rank = jnp.cumsum(is_live, axis=1) - is_live
    slot_index = jnp.arange(block_total, dtype=jnp.int32)
    chosen = (block_rank[:, :, None] == slot_index[None, None, :]) & (is_live[:, :, None] > 0)
    chosen_int = chosen.astype(jnp.int32)
    block_of = jnp.sum(chosen_int * slot_index[None, :, None], axis=1)
    length_of = jnp.sum(chosen_int * block_lengths[:, :, None], axis=1)
    return (counts, prefix, block_rank, block_of, length_of)


def layer(inputs, work_len, w_in, w_out):
    block_count = inputs.shape[0]
    block_len = inputs.shape[1]
    model_width = inputs.shape[2]
    attn_width = w_out.shape[0]
    head_count = attn_width // HD
    floated = inputs.astype(jnp.float32)
    row_mean = jnp.mean(floated, axis=-1, keepdims=True)
    centred = floated - row_mean
    row_var = jnp.mean(centred * centred, axis=-1, keepdims=True)
    normed = (centred * lax.rsqrt(row_var + EPSILON)).astype(jnp.bfloat16)
    projected = jnp.dot(normed.reshape(-1, model_width), w_in, preferred_element_type=jnp.float32)
    activated = jax.nn.silu(projected).astype(jnp.bfloat16)
    gating = activated[:, :attn_width]
    values = activated[:, attn_width : 2 * attn_width].reshape(
        block_count, block_len, head_count, HD
    )
    queries = activated[:, 2 * attn_width : 3 * attn_width].reshape(
        block_count, block_len, head_count, HD
    )
    key_rows = activated[:, 3 * attn_width :].reshape(block_count, block_len, head_count, HD)
    scores = jnp.einsum(
        "bihd,bjhd->bhij", queries.astype(jnp.float32), key_rows.astype(jnp.float32)
    ) * HD ** (-0.5)
    position = jnp.arange(block_len, dtype=jnp.int32)
    causal = position[None, :] <= position[:, None]
    limit = work_len[:, None, None, None]
    allowed = (
        causal[None, None, :, :]
        & (position[None, None, None, :] < limit)
        & (position[None, None, :, None] < limit)
    )
    weights = jnp.where(allowed, jax.nn.silu(scores), 0.0).astype(jnp.bfloat16)
    mixed = jnp.einsum("bhij,bjhd->bihd", weights.astype(jnp.float32), values.astype(jnp.float32))
    mixed = mixed.reshape(block_count * block_len, attn_width)
    mix_mean = jnp.mean(mixed, axis=-1, keepdims=True)
    mix_centred = mixed - mix_mean
    mix_var = jnp.mean(mix_centred * mix_centred, axis=-1, keepdims=True)
    gated = (
        mix_centred * lax.rsqrt(jnp.maximum(mix_var, MIX_FLOOR)) * gating.astype(jnp.float32)
    ).astype(jnp.bfloat16)
    output = floated.reshape(-1, model_width) + jnp.dot(
        gated, w_out, preferred_element_type=jnp.float32
    )
    rows_ok = (position[None, :] < work_len[:, None]).reshape(-1, 1)
    result = (
        jnp.where(rows_ok, output, 0.0)
        .astype(jnp.bfloat16)
        .reshape(block_count, block_len, model_width)
    )
    return (result, gated)


def shards(embed, lengths, w_in, w_out, cotangent):
    peer_count = lax.axis_size("peer")
    group_total = lax.axis_size("group")
    own_peer = lax.axis_index("peer")
    model_width = embed.shape[1]
    blocks = lengths.shape[1] // peer_count
    pair_depth = (blocks + peer_count - 1) // peer_count
    work_slots = cotangent.shape[0] // BLK
    block_lengths = lengths[0].reshape(peer_count, blocks)
    counts, prefix, block_rank, block_of, length_of = plan_tables(block_lengths)
    own_prefix = prefix[own_peer]
    own_count = counts[own_peer]
    dest_index = jnp.arange(peer_count, dtype=jnp.int32)
    pair_index = jnp.arange(pair_depth, dtype=jnp.int32)
    offset = ((dest_index - own_prefix) % peer_count)[:, None] + pair_index[None, :] * peer_count
    is_valid = offset < own_count
    picked = block_of[own_peer][jnp.minimum(offset, blocks - 1)]
    home_rows = embed.reshape(blocks, BLK, model_width)
    outgoing = jnp.where(is_valid[:, :, None, None], home_rows[picked], jnp.zeros((), embed.dtype))
    arrived = lax.all_to_all(
        outgoing.reshape(peer_count, pair_depth * BLK, model_width),
        "peer",
        split_axis=0,
        concat_axis=0,
        tiled=True,
    )
    arrived = arrived.reshape(peer_count, pair_depth, BLK, model_width)
    ticket = jnp.arange(work_slots, dtype=jnp.int32) * peer_count + own_peer
    source_end = prefix + counts
    source = jnp.sum((source_end[None, :] <= ticket[:, None]).astype(jnp.int32), axis=1)
    source = jnp.minimum(source, peer_count - 1)
    within = jnp.clip(ticket - prefix[source], 0, blocks - 1)
    work_len = length_of[source, within]
    work_rows = arrived[source, jnp.minimum(within // peer_count, pair_depth - 1)]
    result, pullback, gated = jax.vjp(
        lambda inputs: layer(inputs, work_len, w_in, w_out), work_rows, has_aux=True
    )
    cotan_blocks = cotangent.reshape(work_slots, BLK, model_width)
    (grad_work,) = pullback(cotan_blocks)
    back_offset = ((own_peer - prefix) % peer_count)[:, None] + pair_index[None, :] * peer_count
    back_valid = back_offset < counts[:, None]
    back_slot = jnp.clip((prefix[:, None] + back_offset) // peer_count, 0, work_slots - 1)
    returning = jnp.where(
        back_valid[:, :, None, None], grad_work[back_slot], jnp.zeros((), grad_work.dtype)
    )
    returned = lax.all_to_all(
        shortened(returning.reshape(peer_count, pair_depth * BLK, model_width)),
        "peer",
        split_axis=0,
        concat_axis=0,
        tiled=True,
    )
    returned = returned.reshape(peer_count, pair_depth, BLK, model_width)
    own_rank = block_rank[own_peer]
    target = (own_prefix + own_rank) % peer_count
    own_live = block_lengths[own_peer] > 0
    grad_back = jnp.where(
        own_live[:, None, None],
        returned[target, jnp.minimum(own_rank // peer_count, pair_depth - 1)],
        jnp.zeros((), returned.dtype),
    )
    attn_width = w_out.shape[0]
    grad_scale = 1.0 / math.sqrt(group_total * peer_count * work_slots * BLK)
    columns = lax.slice_in_dim(gated, 0, attn_width // peer_count * lax.axis_size("peer"), axis=1)
    grad_share = lax.psum_scatter(
        lax.dot_general(
            columns, cotangent, (((0,), (0,)), ((), ())), preferred_element_type=jnp.float32
        )
        * grad_scale,
        "peer",
        scatter_dimension=0,
        tiled=True,
    )
    grad_piece = lax.psum_scatter(grad_share, "group", scatter_dimension=1, tiled=True)
    return (result.reshape(-1, model_width), grad_back.reshape(-1, model_width), grad_piece)


def solution(mesh):
    placed = (P(("group", "peer"), None), P("group", None), P(), P(), P(("group", "peer"), None))
    return jax.shard_map(
        shards,
        mesh=mesh,
        in_specs=placed,
        out_specs=(P(("group", "peer"), None), P(("group", "peer"), None), P("peer", "group")),
        check_vma=False,
    )
```

profile of v0, /device:TPU:0, one launch (start us, length us, event | category | flops | bytes accessed | tf_op | source)
XLA Modules:
  0.0 126.1 jit_solution(14982252484215067503)
XLA Ops:
  7.2 0.5 broadcast.1016
  7.7 1.3 %reduce.7 = s32[512]{0:T(512)S(1)} reduce(s32[1,512]{1,0:T(1,128)} %param.6, s32[]{:T(128)} %broadcast.1016), dimensions={0}, to_apply=%param.6.reduce_sub_computation.3 | reduce | bytes 4100 | tf_op args[1]
  9.1 0.1 convert_reduce_fusion.1
  9.2 0.6 dynamic_slice.16
  9.8 0.2 reduce-window.7
  10.0 0.6 dynamic_slice.15
  10.6 0.6 and_select_fusion.4
  11.3 0.7 add_compare_fusion
  12.1 0.2 reduce_window_sum.18
  12.3 0.3 select_reduce_fusion.1
  12.7 0.8 gather_fusion.2
  13.8 0.6 gather_fusion.3
  14.4 1.1 bitcast_select_fusion.2
  15.6 5.2 %all-to-all-start = ((bf16[8,64,1024]{2,1,0:T(8,128)(2,1)}), bf16[8,64,1024]{2,1,0:T(8,128)(2,1)S(1)}, u32[]{:S(2)}, u32[]{:S(2)}) async-start(bf16[8,64,1024]{2,1,0:T(8,128)(2,1)} %bitcast_select_fusion.2), calls=%async_computation | async-start | bytes 2097152 | tf_op jit(solution)/shard_map/all_to_all | solution.py:110
  20.9 0.7 gather_fusion
  21.6 0.7 gather_fusion.1
  22.4 0.1 lt.179
  22.8 0.1 and_and_fusion
  22.9 13.3 %all-to-all-done = bf16[8,64,1024]{2,1,0:T(8,128)(2,1)S(1)} async-done(((bf16[8,64,1024]{2,1,0:T(8,128)(2,1)}), bf16[8,64,1024]{2,1,0:T(8,128)(2,1)S(1)}, u32[]{:S(2)}, u32[]{:S(2)}) %all-to-all-start) | async-done | bytes 1048608 | tf_op jit(solution)/shard_map/all_to_all | solution.py:110
  36.1 0.6 gather_fusion.4
  36.8 0.1 convert_reduce_fusion
  37.0 0.3 fusion.21
  37.4 4.9 %multiply_convert_fusion = (bf16[256,2048]{1,0:T(8,128)(2,1)S(1)}, f32[256,2048]{1,0:T(8,128)}) fusion(bf16[1024,2048]{1,0:T(8,128)(2,1)} %param.7, bf16[32,8,1024]{2,1,0:T(8,128)(2,1)S(1)} %gather_fusion.4, f32[256]{0:T(256)S(1)} %rsqrt.24, f32[256]{0:T(256)S(1)} %div.96), kind=kOutput, calls=%fused_computation.13 | convolution fusion | flops 1077411840 | bytes 7866368 | tf_op jit(solution)/shard_map/jvp()/dot_general | solution.py:49
  42.3 0.3 convolution_multiply_fusion.1
  42.6 0.7 copy-done.2
  43.3 0.4 bitcast_reduce_fusion
  43.8 0.2 fusion.46
  44.2 0.2 copy-done.1
  44.4 1.9 %multiply_reduce_fusion = (f32[256]{0:T(256)S(1)}, f32[256,512]{1,0:T(8,128)S(1)}) fusion(f32[32,4,128,8]{2,3,1,0:T(8,128)S(1)} %get-tuple-element.30, f32[256]{0:T(256)S(1)} %div.101, bf16[256,2048]{1,0:T(8,128)(2,1)} %copy-done.2, bf16[512,1024]{1,0:T(8,128)(2,1)} %param.8, bf16[256,1024]{1,0:T(8,128)(2,1)S(1)} %copy-done.1, pred[256]{0:T(512)(128)(4,1)S(1)} %lt.179), kind=kOutput, calls=%fused_computation.82 | convolution fusion | flops 269876992 | bytes 2885888 | tf_op jit(solution)/shard_map/transpose(jvp())/dot_general | solution.py:79
  46.3 1.0 fusion.88
  47.3 0.4 fusion.40
  47.7 1.0 fusion.19
  48.7 1.8 %convolution_multiply_fusion = f32[512,1024]{1,0:T(8,128)} fusion(bf16[256,512]{1,0:T(8,128)(2,1)S(1)} %get-tuple-element.11, bf16[256,1024]{1,0:T(8,128)(2,1)S(1)} %copy-done.1), kind=kOutput, calls=%fused_computation.15 | convolution fusion | flops 268959744 | bytes 2883584 | tf_op jit(solution)/shard_map/dot_general | solution.py:156
  50.5 1.5 %fusion.18 = bf16[256,512]{1,0:T(8,128)(2,1)S(1)} fusion(bf16[32,4,8,8]{3,2,1,0:T(8,128)(2,1)S(1)} %fusion.40, bf16[256,2048]{1,0:T(8,128)(2,1)} %copy-done.2), kind=kOutput, calls=%fused_computation.42 | convolution fusion | flops 2097152 | bytes 540672 | tf_op jit(solution)/shard_map/transpose(jvp(bihd,bjhd->bhij))/dot_general | solution.py:59
  52.0 1.5 %fusion.20 = bf16[256,512]{1,0:T(8,128)(2,1)S(1)} fusion(f32[256,512]{1,0:T(8,128)} %copy-done.4, f32[256]{0:T(256)S(1)} %negate_multiply_fusion.1, f32[32,4,8,8]{3,2,1,0:T(8,128)S(1)} %convolution_multiply_fusion.1, pred[32,8,8]{2,1,0:T(8,128)(4,1)S(1)} %and_and_fusion), kind=kOutput, calls=%fused_computation.44 | convolution fusion | flops 2408448 | bytes 822272 | tf_op jit(solution)/shard_map/transpose(jvp(bhij,bjhd->bihd))/dot_general | solution.py:71
  53.5 4.1 %fusion.28 = (f32[256]{0:T(256)S(1)}, bf16[256,1024]{1,0:T(8,128)(2,1)S(1)}) fusion(bf16[32,8,1024]{2,1,0:T(8,128)(2,1)S(1)} %gather_fusion.4, f32[256]{0:T(256)S(1)} %div.96, bf16[1024,2048]{1,0:T(8,128)(2,1)} %param.7, f32[256,2048]{1,0:T(8,128)S(1)} %copy-done.7, bf16[256,512]{1,0:T(8,128)(2,1)S(1)} %copy-done.5, bf16[256,512]{1,0:T(8,128)(2,1)S(1)} %fusion.20, ...), kind=kOutput, calls=%fused_computation.52 | convolution fusion | flops 1084227328 | bytes 8390656 | tf_op jit(solution)/shard_map/transpose(jvp())/dot_general | solution.py:49
  57.7 0.4 fusion.26
  58.3 0.5 fusion.25
  58.8 0.6 gather_fusion.5
  59.4 1.1 bitcast_select_fusion.1
  60.5 3.6 %all-to-all-start.1 = ((bf16[8,64,1024]{2,1,0:T(8,128)(2,1)}), bf16[8,64,1024]{2,1,0:T(8,128)(2,1)S(1)}, u32[]{:S(2)}, u32[]{:S(2)}) async-start(bf16[8,64,1024]{2,1,0:T(8,128)(2,1)} %bitcast_select_fusion.1), calls=%async_computation.1 | async-start | bytes 2097152 | tf_op jit(solution)/shard_map/all_to_all | solution.py:136
  64.2 0.1 broadcast_in_dim.136
  64.3 0.6 fusion.80
  65.0 31.7 %reduce-scatter.3.cloned.1.call-done = f32[64,1024]{1,0:T(8,128)} async-done(((f32[512,1024]{1,0:T(8,128)}), f32[64,1024]{1,0:T(8,128)}) %reduce-scatter.3.cloned.1.call-update) | async-done | bytes 262160 | tf_op jit(solution)/shard_map/reduce_scatter | solution.py:155
  96.7 2.5 %fusion.9 = bf16[256,1024]{1,0:T(8,128)(2,1)} fusion(bf16[256,512]{1,0:T(8,128)(2,1)S(1)} %get-tuple-element.11, bf16[512,1024]{1,0:T(8,128)(2,1)} %param.8, bf16[32,8,1024]{2,1,0:T(8,128)(2,1)S(1)} %gather_fusion.4, pred[256]{0:T(512)(128)(4,1)S(1)} %lt.179), kind=kOutput, calls=%fused_computation.29 | convolution fusion | flops 269484032 | bytes 2359552 | tf_op jit(solution)/shard_map/jvp()/dot_general | solution.py:79
  99.2 0.7 gather_fusion.6
  99.9 1.1 bitcast_select_fusion
  101.0 18.2 %reduce-scatter.5.cloned.1.call-done = f32[64,256]{1,0:T(8,128)} async-done(((f32[64,1024]{1,0:T(8,128)}), f32[64,256]{1,0:T(8,128)}) %reduce-scatter.5.cloned.1.call-update) | async-done | bytes 65552 | tf_op jit(solution)/shard_map/reduce_scatter | solution.py:164
  (63 shorter events, 2.0 us)
Async XLA Ops:
  7.2 6.7 %copy-start = (bf16[512,1024]{1,0:T(8,128)(2,1)S(1)}, bf16[512,1024]{1,0:T(8,128)(2,1)}, u32[]{:S(2)}) copy-start(bf16[512,1024]{1,0:T(8,128)(2,1)} %param.5) | copy-start | bytes 3145732
  15.6 20.6 %all-to-all-start = ((bf16[8,64,1024]{2,1,0:T(8,128)(2,1)}), bf16[8,64,1024]{2,1,0:T(8,128)(2,1)S(1)}, u32[]{:S(2)}, u32[]{:S(2)}) async-start(bf16[8,64,1024]{2,1,0:T(8,128)(2,1)} %bitcast_select_fusion.2), calls=%async_computation | async-start | bytes 2097152 | tf_op jit(solution)/shard_map/all_to_all | solution.py:110
  20.7 76.0 %reduce-scatter.3.cloned.1.call-start = ((), (), s32[]{:S(2)}) async-start(), calls=%async_computation.4 | async-start | bytes 2359296 | tf_op jit(solution)/shard_map/reduce_scatter | solution.py:155
  42.3 1.0 copy-start.2
  43.3 1.0 copy-start.1
  44.4 2.0 %copy-start.3 = (bf16[256,2048]{1,0:T(8,128)(2,1)S(1)}, bf16[256,2048]{1,0:T(8,128)(2,1)}, u32[]{:S(2)}) copy-start(bf16[256,2048]{1,0:T(8,128)(2,1)} %copy-done.2) | copy-start | bytes 3145732
  47.3 1.4 %copy-start.4 = (f32[256,512]{1,0:T(8,128)}, f32[256,512]{1,0:T(8,128)S(1)}, u32[]{:S(2)}) copy-start(f32[256,512]{1,0:T(8,128)S(1)} %get-tuple-element.8) | copy-start | bytes 1572868
  50.5 3.0 %copy-start.5 = (bf16[256,512]{1,0:T(8,128)(2,1)S(1)}, bf16[256,512]{1,0:T(8,128)(2,1)}, u32[]{:S(2)}) copy-start(bf16[256,512]{1,0:T(8,128)(2,1)} %get-tuple-element.12) | copy-start | bytes 786436
  50.5 3.0 %copy-start.6 = (bf16[256,512]{1,0:T(8,128)(2,1)S(1)}, bf16[256,512]{1,0:T(8,128)(2,1)}, u32[]{:S(2)}) copy-start(bf16[256,512]{1,0:T(8,128)(2,1)} %fusion.19) | copy-start | bytes 786436
  50.5 3.0 %copy-start.7 = (f32[256,2048]{1,0:T(8,128)S(1)}, f32[256,2048]{1,0:T(8,128)}, u32[]{:S(2)}) copy-start(f32[256,2048]{1,0:T(8,128)} %get-tuple-element.28) | copy-start | bytes 6291460
  60.5 38.7 %all-to-all-start.1 = ((bf16[8,64,1024]{2,1,0:T(8,128)(2,1)}), bf16[8,64,1024]{2,1,0:T(8,128)(2,1)S(1)}, u32[]{:S(2)}, u32[]{:S(2)}) async-start(bf16[8,64,1024]{2,1,0:T(8,128)(2,1)} %bitcast_select_fusion.1), calls=%async_computation.1 | async-start | bytes 2097152 | tf_op jit(solution)/shard_map/all_to_all | solution.py:136
  64.1 55.1 %reduce-scatter.5.cloned.1.call-start = ((), (), s32[]{:S(2)}) async-start(), calls=%async_computation.5 | async-start | bytes 327680 | tf_op jit(solution)/shard_map/reduce_scatter | solution.py:164
Sparse Core Ops, SparseCore 0:
  50.6 46.0 reduce-scatter.2
  99.6 19.5 reduce-scatter.4
where the time goes:
time: 127 us; the launch traced here: 126 us
  waiting for transfers between devices  63.2 us (50%)
  matrix products  20.2 us (16%)
  between operations  14.3 us (11%)
  other arithmetic  10.5 us (8%)
  local copies, waits for them, and re-layouts  8.92 us (7%)
  starting transfers between devices  8.81 us (7%)
    reduce_scatter x1, waiting for transfers between devices, shards(): lax.psum_scatter(lax.dot_general(columns, cotangent, (((0,), (0,)), ((),...  31.7 us
    reduce_scatter x1, waiting for transfers between devices, shards(): lax.psum_scatter(grad_share, 'group', scatter_dimension=1, tiled=True)  18.2 us
    all_to_all x1, waiting for transfers between devices, shards(): lax.all_to_all(outgoing.reshape(peer_count, pair_depth * BLK, model_width...  13.3 us
    dot_general x2, matrix products, layer(): jnp.dot(normed.reshape(-1, model_width), w_in, preferred_element_type=jnp...  9.06 us
    all_to_all x1, starting transfers between devices, shards(): lax.all_to_all(outgoing.reshape(peer_count, pair_depth * BLK, model_width...  5.17 us
    dot_general x2, matrix products, layer(): jnp.dot(gated, w_out, preferred_element_type=jnp.float32)  4.43 us
    all_to_all x1, starting transfers between devices, shards(): lax.all_to_all(shortened(returning.reshape(peer_count, pair_depth * BLK,...  3.56 us
    dot_general x3, matrix products, layer(): jnp.einsum('bihd,bjhd->bhij', queries.astype(jnp.float32), key_rows.astyp...  2.72 us
  transfers between devices with their start and end apart: 4, of which 3 were waited for; matrix products, arithmetic and copies ran while one was open for 14% of the time, Pallas kernels for 0%

commit v1 on v0

--- a/solution.py
+++ b/solution.py
@@ -1,8 +1,11 @@
+import functools
 import math
 
 import jax
 import jax.numpy as jnp
 from jax import lax
+from jax.experimental import pallas as pl
+from jax.experimental.pallas import tpu as pltpu
 from jax.sharding import PartitionSpec as P
 
 HD = 128
@@ -165,12 +168,583 @@
     return (result.reshape(-1, model_width), grad_back.reshape(-1, model_width), grad_piece)
 
 
+MESH = pl.DeviceIdType.MESH
+F32 = jnp.float32
+BF16 = jnp.bfloat16
+NT = (((1,), (1,)), ((), ()))
+TN = (((0,), (0,)), ((), ()))
+
+
+def toggled(index, bits):
+    result = index
+    bit = 1
+    while bit <= bits:
+        if bits & bit:
+            result = result + bit * (1 - 2 * lax.rem(lax.div(index, bit), 2))
+        bit *= 2
+    return result
+
+
+def dotf(a, b, dims=None):
+    if dims is None:
+        return jnp.dot(a, b, preferred_element_type=F32)
+    return lax.dot_general(a, b, dims, preferred_element_type=F32)
+
+
+def fused(
+    peers,
+    groups,
+    len_ref,
+    embed_hbm,
+    w_in_hbm,
+    w_out_hbm,
+    cot_hbm,
+    out_ref,
+    grad_ref,
+    gproj_ref,
+    cot_v,
+    embed_v,
+    w_in_v,
+    w_out_v,
+    csend,
+    crecv,
+    osend,
+    orecv,
+    take_ref,
+    pack_ref,
+    x_ref,
+    nrm_ref,
+    inv_ref,
+    act_ref,
+    der_ref,
+    wts_ref,
+    dsw_ref,
+    y_ref,
+    gated_ref,
+    inv2_ref,
+    flag_ref,
+    valid_ref,
+    dg_ref,
+    dproj_ref,
+    dn_ref,
+    gradp_ref,
+    gfull_ref,
+    core_send,
+    core_recv,
+    held_ref,
+    z_send,
+    z_recv,
+    p_send,
+    p_recv,
+    in_sem,
+    cs_sem,
+    cr_sem,
+    os_sem,
+    or_sem,
+    core_sem,
+    zs_sem,
+    zr_sem,
+    ps_sem,
+    pr_sem,
+):
+    me = lax.axis_index("peer")
+    grp = lax.axis_index("group")
+    rows, width = embed_v.shape
+    work_rows = cot_v.shape[0]
+    attn = w_out_v.shape[0]
+    heads = attn // HD
+    chunk = rows // peers
+    blocks = rows // BLK
+    total = len_ref.shape[1]
+    tile = min(rows, 256)
+    tiles = rows // tile
+    per_tile = tile // chunk
+    bit_count = peers.bit_length() - 1
+    col = 256
+    part = attn // peers
+    gcols = width // groups
+    half = peers // 2
+
+    barrier = pltpu.get_barrier_semaphore()
+    for j in range(1, peers):
+        pl.semaphore_signal(
+            barrier, inc=1, device_id={"peer": toggled(me, j)}, device_id_type=MESH
+        )
+    for d in range(1, groups):
+        pl.semaphore_signal(
+            barrier, inc=1, device_id={"group": lax.rem(grp + d, groups)}, device_id_type=MESH
+        )
+
+    loads = []
+    for place, (src, dst) in enumerate(
+        ((cot_hbm, cot_v), (embed_hbm, embed_v), (w_in_hbm, w_in_v), (w_out_hbm, w_out_v))
+    ):
+        load = pltpu.make_async_copy(src, dst, in_sem.at[place])
+        load.start()
+        loads.append(load)
+
+    lens = len_ref[...]
+    live = jnp.where(lens > 0, 1.0, 0.0).astype(F32)
+    lane = lax.broadcasted_iota(jnp.int32, (1, total), 1)
+    before = (
+        lax.broadcasted_iota(jnp.int32, (total, total), 0)
+        < lax.broadcasted_iota(jnp.int32, (total, total), 1)
+    )
+    before = jnp.where(before, 1.0, 0.0).astype(BF16)
+    ticket = dotf(jnp.broadcast_to(live, (16, total)).astype(BF16), before).astype(jnp.int32)
+    peer_end = (
+        lax.broadcasted_iota(jnp.int32, (peers, total), 1)
+        < (lax.broadcasted_iota(jnp.int32, (peers, total), 0) + 1) * blocks
+    )
+    ends = jnp.sum(jnp.where(peer_end, live, 0.0), axis=1, keepdims=True).astype(jnp.int32)
+    own_prefix = jnp.sum(jnp.where(lane < me * blocks, live, 0.0), axis=1, keepdims=True).astype(
+        jnp.int32
+    )
+
+    wlane = lax.broadcasted_iota(jnp.int32, (1, work_rows), 1)
+    wticket = lax.shift_right_logical(wlane, 3) * peers + me
+    passed = ends <= wticket
+    source = jnp.sum(jnp.where(passed, 1, 0), axis=0, keepdims=True)
+    start = jnp.max(jnp.where(passed, ends, 0), axis=0, keepdims=True)
+    depth = lax.shift_right_logical(wticket - start, bit_count)
+    wtarget = (source ^ me) * chunk + depth * BLK + (wlane & (BLK - 1))
+    pack_ref[...] = jnp.where(
+        lax.broadcasted_iota(jnp.int32, (rows, work_rows), 0) == wtarget, 1.0, 0.0
+    ).astype(BF16)
+
+    loads[0].wait()
+
+    def pack(n, _):
+        cols = pl.ds(pl.multiple_of(n * col, col), col)
+        csend[:, cols] = dotf(pack_ref[...], cot_v[:, cols]).astype(BF16)
+        return 0
+
+    lax.fori_loop(0, width // col, pack, 0)
+    pl.semaphore_wait(barrier, peers - 1 + groups - 1)
+
+    def exchange(src, dst, s_sem, r_sem, j):
+        span = pl.ds(j * chunk, chunk)
+        return pltpu.make_async_remote_copy(
+            src_ref=src.at[span],
+            dst_ref=dst.at[span],
+            send_sem=s_sem.at[j],
+            recv_sem=r_sem.at[j],
+            device_id={"peer": toggled(me, j)},
+            device_id_type=MESH,
+        )
+
+    cot_moves = {j: exchange(csend, crecv, cs_sem, cr_sem, j) for j in range(1, peers)}
+    for j in reversed(range(1, peers)):
+        cot_moves[j].start()
+    crecv[pl.ds(0, chunk), :] = csend[pl.ds(0, chunk), :]
+
+    spot = lax.broadcasted_iota(jnp.int32, (16, total), 0)
+    high = lax.shift_right_logical(ticket, 7)
+    low = ticket & 127
+    facts = jnp.where(spot == 0, high, jnp.where(spot == 1, low, lens)).astype(F32).astype(BF16)
+    spread = (
+        lax.broadcasted_iota(jnp.int32, (total, rows), 0)
+        == me * blocks + lax.shift_right_logical(lax.broadcasted_iota(jnp.int32, (total, rows), 1), 3)
+    )
+    facts = dotf(facts, jnp.where(spread, 1.0, 0.0).astype(BF16)).astype(jnp.int32)
+    hticket = facts[0:1] * 128 + facts[1:2]
+    hlen = facts[2:3]
+    hlane = lax.broadcasted_iota(jnp.int32, (1, rows), 1)
+    rank = hticket - own_prefix
+    target = (
+        ((hticket & (peers - 1)) ^ me) * chunk
+        + lax.shift_right_logical(rank, bit_count) * BLK
+        + (hlane & (BLK - 1))
+    )
+    target = jnp.where(hlen > 0, target, -1)
+    chosen = lax.broadcasted_iota(jnp.int32, (rows, rows), 0) == target
+    take_ref[...] = jnp.where(chosen, 1.0, 0.0).astype(BF16)
+    slot_len = jnp.sum(
+        jnp.where(chosen, hlen.astype(F32), 0.0), axis=1, keepdims=True
+    )
+    row_in = lax.broadcasted_iota(jnp.int32, (rows, 1), 0) & (BLK - 1)
+    valid_ref[...] = jnp.where(row_in.astype(F32) < slot_len, 1.0, 0.0)
+
+    out_moves = {j: exchange(osend, orecv, os_sem, or_sem, j) for j in range(1, peers)}
+    small = 32
+    scale = HD ** (-0.5)
+    sub = min(tile, 128)
+    si = lax.broadcasted_iota(jnp.int32, (sub, sub), 0)
+    sj = lax.broadcasted_iota(jnp.int32, (sub, sub), 1)
+    near = (lax.shift_right_logical(si, 3) == lax.shift_right_logical(sj, 3)) & (sj <= si)
+    near = jnp.where(near, 1.0, 0.0)
+
+    loads[1].wait()
+    for place, t in enumerate(reversed(range(tiles))):
+        span = pl.ds(t * tile, tile)
+
+        def pick(n, _):
+            cols = pl.ds(pl.multiple_of(n * col, col), col)
+            x_ref[span, cols] = dotf(take_ref[span, :], embed_v[:, cols]).astype(BF16)
+            return 0
+
+        lax.fori_loop(0, width // col, pick, 0)
+
+        def norm(s, _):
+            part_rows = pl.ds(pl.multiple_of(t * tile + s * small, small), small)
+            x = x_ref[part_rows, :].astype(F32)
+            x = x - jnp.mean(x, axis=1, keepdims=True)
+            inv = lax.rsqrt(jnp.mean(x * x, axis=1, keepdims=True) + EPSILON)
+            nrm_ref[part_rows, :] = (x * inv).astype(BF16)
+            inv_ref[part_rows, :] = inv
+            return 0
+
+        lax.fori_loop(0, tile // small, norm, 0)
+        if place == 0:
+            loads[2].wait()
+
+        def project(n, _):
+            cols = pl.ds(pl.multiple_of(n * col, col), col)
+            v = dotf(nrm_ref[span, :], w_in_v[:, cols])
+            sig = 0.5 * jnp.tanh(0.5 * v) + 0.5
+            act = v * sig
+            act_ref[span, cols] = act.astype(BF16)
+            der_ref[span, cols] = (sig + act * (1.0 - sig)).astype(BF16)
+            return 0
+
+        lax.fori_loop(0, 4 * attn // col, project, 0)
+
+        def attend(s, _):
+            sr = pl.ds(pl.multiple_of(t * tile + s * sub, sub), sub)
+            allowed = near * valid_ref[sr, :]
+            mixed = []
+            for h in range(heads):
+                hc = pl.ds(h * HD, HD)
+                values = act_ref[sr, pl.ds(attn + h * HD, HD)]
+                queries = act_ref[sr, pl.ds(2 * attn + h * HD, HD)]
+                keys = act_ref[sr, pl.ds(3 * attn + h * HD, HD)]
+                score = dotf(queries, keys, NT) * scale
+                sig = 0.5 * jnp.tanh(0.5 * score) + 0.5
+                weight = score * sig
+                slope = (sig + weight * (1.0 - sig)) * scale
+                weight = jnp.where(allowed > 0.0, weight, 0.0).astype(BF16)
+                wts_ref[sr, pl.ds(h * sub, sub)] = weight
+                dsw_ref[sr, pl.ds(h * sub, sub)] = jnp.where(allowed > 0.0, slope, 0.0).astype(BF16)
+                mixed.append(dotf(weight, values))
+            mixed = jnp.concatenate(mixed, axis=1)
+            mixed = mixed - jnp.mean(mixed, axis=1, keepdims=True)
+            var = jnp.mean(mixed * mixed, axis=1, keepdims=True)
+            inv = lax.rsqrt(jnp.maximum(var, MIX_FLOOR))
+            y = mixed * inv
+            inv2_ref[sr, :] = inv
+            flag_ref[sr, :] = jnp.where(
+                var > MIX_FLOOR, 1.0, jnp.where(var == MIX_FLOOR, 0.5, 0.0)
+            )
+            y_ref[sr, :] = y.astype(BF16)
+            gated_ref[sr, :] = (y * act_ref[sr, pl.ds(0, attn)].astype(F32)).astype(BF16)
+            return 0
+
+        lax.fori_loop(0, tile // sub, attend, 0)
+        if place == 0:
+            loads[3].wait()
+
+        def produce(n, _):
+            cols = pl.ds(pl.multiple_of(n * col, col), col)
+            out = x_ref[span, cols].astype(F32) + dotf(gated_ref[span, :], w_out_v[:, cols])
+            osend[span, cols] = jnp.where(valid_ref[span, :] > 0.0, out, 0.0).astype(BF16)
+            return 0
+
+        lax.fori_loop(0, width // col, produce, 0)
+        for j in reversed(range(t * per_tile, (t + 1) * per_tile)):
+            if j:
+                out_moves[j].start()
+    orecv[pl.ds(0, chunk), :] = osend[pl.ds(0, chunk), :]
+
+    for j in range(1, peers):
+        cot_moves[j].wait_recv()
+
+    def mask(s, _):
+        sr = pl.ds(pl.multiple_of(s * small, small), small)
+        got = crecv[sr, :].astype(F32)
+        crecv[sr, :] = jnp.where(valid_ref[sr, :] > 0.0, got, 0.0).astype(BF16)
+        return 0
+
+    lax.fori_loop(0, rows // small, mask, 0)
+
+    def outer(n, _):
+        cols = pl.ds(pl.multiple_of(n * col, col), col)
+        gfull_ref[:, cols] = dotf(gated_ref[...], crecv[:, cols], TN)
+        return 0
+
+    lax.fori_loop(0, width // col, outer, 0)
+    for m in range(half):
+        theirs = pl.multiple_of(toggled(me, 2 * m + 1) * part, part)
+        core_send[pl.ds(m * part, part), :] = gfull_ref[pl.ds(theirs, part), :].astype(BF16)
+    core_move = pltpu.make_async_remote_copy(
+        src_ref=core_send,
+        dst_ref=core_recv,
+        send_sem=core_sem.at[0],
+        recv_sem=core_sem.at[1],
+        device_id={"peer": toggled(me, 1)},
+        device_id_type=MESH,
+    )
+    core_move.start()
+
+    def backward(t):
+        span = pl.ds(t * tile, tile)
+
+        def back_out(n, _):
+            cols = pl.ds(pl.multiple_of(n * col, col), col)
+            dg_ref[:, cols] = dotf(crecv[span, :], w_out_v[cols, :], NT).astype(BF16)
+            return 0
+
+        lax.fori_loop(0, attn // col, back_out, 0)
+
+        def back_attend(s, _):
+            here = pl.ds(pl.multiple_of(s * sub, sub), sub)
+            sr = pl.ds(pl.multiple_of(t * tile + s * sub, sub), sub)
+            dg = dg_ref[here, :].astype(F32)
+            y = y_ref[sr, :].astype(F32)
+            gate = pl.ds(0, attn)
+            dgate = (dg * y).astype(BF16).astype(F32)
+            dproj_ref[here, gate] = (dgate * der_ref[sr, gate].astype(F32)).astype(BF16)
+            dy = dg * act_ref[sr, gate].astype(F32)
+            slant = jnp.mean(dy * y, axis=1, keepdims=True) * flag_ref[sr, :]
+            dc = (dy - y * slant) * inv2_ref[sr, :]
+            dmix = (dc - jnp.mean(dc, axis=1, keepdims=True)).astype(BF16)
+            for h in range(heads):
+                vc = pl.ds(attn + h * HD, HD)
+                qc = pl.ds(2 * attn + h * HD, HD)
+                kc = pl.ds(3 * attn + h * HD, HD)
+                dm = dmix[:, h * HD : (h + 1) * HD]
+                dw = dotf(dm, act_ref[sr, vc], NT).astype(BF16).astype(F32)
+                ds = (dw * dsw_ref[sr, pl.ds(h * sub, sub)].astype(F32)).astype(BF16)
+                dv = dotf(wts_ref[sr, pl.ds(h * sub, sub)], dm, TN)
+                dq = dotf(ds, act_ref[sr, kc])
+                dk = dotf(ds, act_ref[sr, qc], TN)
+                for place_of, grad in ((vc, dv), (qc, dq), (kc, dk)):
+                    grad = grad.astype(BF16).astype(F32)
+                    dproj_ref[here, place_of] = (grad * der_ref[sr, place_of].astype(F32)).astype(BF16)
+            return 0
+
+        lax.fori_loop(0, tile // sub, back_attend, 0)
+
+        def back_in(n, _):
+            cols = pl.ds(pl.multiple_of(n * col, col), col)
+            dn_ref[:, cols] = dotf(dproj_ref[...], w_in_v[cols, :], NT).astype(BF16)
+            return 0
+
+        lax.fori_loop(0, width // col, back_in, 0)
+
+        def back_norm(s, _):
+            here = pl.ds(pl.multiple_of(s * small, small), small)
+            sr = pl.ds(pl.multiple_of(t * tile + s * small, small), small)
+            dn = dn_ref[here, :].astype(F32)
+            xh = nrm_ref[sr, :].astype(F32)
+            dc = (dn - xh * jnp.mean(dn * xh, axis=1, keepdims=True)) * inv_ref[sr, :]
+            dx = dc - jnp.mean(dc, axis=1, keepdims=True)
+            gradp_ref[sr, :] = (crecv[sr, :].astype(F32) + dx).astype(BF16)
+            return 0
+
+        lax.fori_loop(0, tile // small, back_norm, 0)
+
+    z_moves = [
+        pltpu.make_async_remote_copy(
+            src_ref=z_send.at[d - 1],
+            dst_ref=z_recv.at[d - 1],
+            send_sem=zs_sem.at[d - 1],
+            recv_sem=zr_sem.at[d - 1],
+            device_id={"group": lax.rem(grp + d, groups)},
+            device_id_type=MESH,
+        )
+        for d in range(1, groups)
+    ]
+    p_moves = [
+        pltpu.make_async_remote_copy(
+            src_ref=p_send.at[m - 1],
+            dst_ref=p_recv.at[m - 1],
+            send_sem=ps_sem.at[m - 1],
+            recv_sem=pr_sem.at[m - 1],
+            device_id={"peer": toggled(me, 2 * m)},
+            device_id_type=MESH,
+        )
+        for m in range(1, half)
+    ]
+    for t in range(tiles):
+        backward(t)
+        if t == 0:
+            core_move.wait_recv()
+            for d in range(groups):
+                theirs = pl.ds(pl.multiple_of(lax.rem(grp + d, groups) * gcols, gcols), gcols)
+                for m in range(half):
+                    ours = pl.multiple_of(toggled(me, 2 * m) * part, part)
+                    mr = pl.ds(m * part, part)
+                    pair = gfull_ref[pl.ds(ours, part), theirs] + core_recv[mr, theirs].astype(F32)
+                    if d:
+                        z_send[d - 1, mr, :] = pair.astype(BF16)
+                    else:
+                        held_ref[mr, :] = pair
+                if d:
+                    z_moves[d - 1].start()
+
+    for move in z_moves:
+        move.wait_recv()
+    for m in reversed(range(half)):
+        mr = pl.ds(m * part, part)
+        share = held_ref[mr, :]
+        for d in range(1, groups):
+            share = share + z_recv[d - 1, mr, :].astype(F32)
+        if m:
+            p_send[m - 1] = share.astype(BF16)
+            p_moves[m - 1].start()
+        else:
+            held_ref[mr, :] = share
+
+    def unpack_grad(n, _):
+        cols = pl.ds(pl.multiple_of(n * col, col), col)
+        grad_ref[:, cols] = dotf(take_ref[...], gradp_ref[:, cols], TN).astype(BF16)
+        return 0
+
+    lax.fori_loop(0, width // col, unpack_grad, 0)
+
+    for j in range(1, peers):
+        out_moves[j].wait_recv()
+
+    def unpack_out(n, _):
+        cols = pl.ds(pl.multiple_of(n * col, col), col)
+        out_ref[:, cols] = dotf(pack_ref[...], orecv[:, cols], TN).astype(BF16)
+        return 0
+
+    lax.fori_loop(0, width // col, unpack_out, 0)
+
+    share = held_ref[pl.ds(0, part), :]
+    for m in range(1, half):
+        p_moves[m - 1].wait_recv()
+        share = share + p_recv[m - 1].astype(F32)
+    gproj_ref[...] = share * (1.0 / math.sqrt(groups * peers * work_rows))
+
+    for j in range(1, peers):
+        cot_moves[j].wait_send()
+        out_moves[j].wait_send()
+    core_move.wait_send()
+    for move in z_moves + p_moves:
+        move.wait_send()
+
+
+def fused_shards(embed, lengths, w_in, w_out, cotangent):
+    peers = lax.axis_size("peer")
+    groups = lax.axis_size("group")
+    rows, width = embed.shape
+    work_rows = cotangent.shape[0]
+    attn = w_out.shape[0]
+    tile = min(rows, 256)
+    sub = min(tile, 128)
+    heads = attn // HD
+    part = attn // peers
+    gcols = width // groups
+    half = peers // 2
+    vmem = pltpu.VMEM
+    dma = pltpu.SemaphoreType.DMA
+    scratch = [
+        vmem((work_rows, width), BF16),
+        vmem((rows, width), BF16),
+        vmem(w_in.shape, BF16),
+        vmem(w_out.shape, BF16),
+        vmem((rows, width), BF16),
+        vmem((rows, width), BF16),
+        vmem((rows, width), BF16),
+        vmem((rows, width), BF16),
+        vmem((rows, rows), BF16),
+        vmem((rows, work_rows), BF16),
+        vmem((rows, width), BF16),
+        vmem((rows, width), BF16),
+        vmem((rows, 1), F32),
+        vmem((rows, 4 * attn), BF16),
+        vmem((rows, 4 * attn), BF16),
+        vmem((rows, heads * sub), BF16),
+        vmem((rows, heads * sub), BF16),
+        vmem((rows, attn), BF16),
+        vmem((rows, attn), BF16),
+        vmem((rows, 1), F32),
+        vmem((rows, 1), F32),
+        vmem((rows, 1), F32),
+        vmem((tile, attn), BF16),
+        vmem((tile, 4 * attn), BF16),
+        vmem((tile, width), BF16),
+        vmem((rows, width), BF16),
+        vmem((attn, width), F32),
+        vmem((half * part, width), BF16),
+        vmem((half * part, width), BF16),
+        vmem((half * part, gcols), F32),
+        vmem((groups - 1, half * part, gcols), BF16),
+        vmem((groups - 1, half * part, gcols), BF16),
+        vmem((half - 1, part, gcols), BF16),
+        vmem((half - 1, part, gcols), BF16),
+        dma((4,)),
+        dma((peers,)),
+        dma((peers,)),
+        dma((peers,)),
+        dma((peers,)),
+        dma((2,)),
+        dma((groups - 1,)),
+        dma((groups - 1,)),
+        dma((half - 1,)),
+        dma((half - 1,)),
+    ]
+    anywhere = pl.BlockSpec(memory_space=pl.ANY)
+    resident = pl.BlockSpec(memory_space=pltpu.VMEM)
+    return pl.pallas_call(
+        functools.partial(fused, peers, groups),
+        out_shape=(
+            jax.ShapeDtypeStruct((work_rows, width), BF16),
+            jax.ShapeDtypeStruct((rows, width), BF16),
+            jax.ShapeDtypeStruct((part, gcols), F32),
+        ),
+        in_specs=[resident] + [anywhere] * 4,
+        out_specs=(resident, resident, resident),
+        scratch_shapes=scratch,
+        compiler_params=pltpu.CompilerParams(
+            collective_id=0, has_side_effects=True, vmem_limit_bytes=48 * 1024 * 1024
+        ),
+        cost_estimate=pl.CostEstimate(
+            flops=2 * rows * width * attn * 11,
+            bytes_accessed=2 * (w_in.size + w_out.size + 3 * rows * width),
+            transcendentals=rows * attn * 5,
+        ),
+    )(lengths, embed, w_in, w_out, cotangent)
+
+
+def fits(mesh):
+    peers = mesh.shape["peer"]
+
+    def check(embed, lengths, w_out):
+        rows = embed.shape[0] // (peers * mesh.shape["group"])
+        part, left = divmod(w_out.shape[0], peers)
+        return (
+            peers & (peers - 1) == 0
+            and peers >= 4
+            and mesh.shape["group"] > 1
+            and rows % (16 * peers) == 0
+            and rows % 256 == 0
+            and 256 % (rows // peers) == 0
+            and left == 0
+            and part % 16 == 0
+            and embed.shape[1] % (256 * mesh.shape["group"]) == 0
+            and lengths.shape[1] * BLK == rows * peers
+        )
+
+    return check
+
+
 def solution(mesh):
     placed = (P(("group", "peer"), None), P("group", None), P(), P(), P(("group", "peer"), None))
-    return jax.shard_map(
-        shards,
-        mesh=mesh,
-        in_specs=placed,
-        out_specs=(P(("group", "peer"), None), P(("group", "peer"), None), P("peer", "group")),
-        check_vma=False,
-    )
+
+    def mapped(body):
+        return jax.shard_map(
+            body,
+            mesh=mesh,
+            in_specs=placed,
+            out_specs=(P(("group", "peer"), None), P(("group", "peer"), None), P("peer", "group")),
+            check_vma=False,
+        )
+
+    def run(embed, lengths, w_in, w_out, cotangent):
+        body = fused_shards if fits(mesh)(embed, lengths, w_out) else shards
+        return mapped(body)(embed, lengths, w_in, w_out, cotangent)
+
+    return run

time: 127 us -> 54.1 us (0.43)
  waiting for transfers between devices: 63.2 us -> 0 us
  Pallas kernels: 0 us -> 46.6 us
  matrix products: 20.2 us -> 0 us
  between operations: 14.3 us -> 0.65 us
  other arithmetic: 10.5 us -> 0 us
  starting transfers between devices: 8.81 us -> 0 us
  local copies, waits for them, and re-layouts: 8.92 us -> 6.56 us
    reduce_scatter x2 -> x0, waiting for transfers between devices: 49.9 us -> none  [the longest x1 31.7 us: shards(): lax.psum_scatter(lax.dot_general(columns, cotangent, (((0,), (0,)), ((),...]
    pallas_call x0 -> x1, Pallas kernels: none -> 46.6 us  [fused_shards(): pl.pallas_call(functools.partial(fused, peers, groups), out_shape=(jax.Sh...]
    dot_general x11 -> x0, matrix products: 20.2 us -> none  [the longest x2 9.06 us: layer(): jnp.dot(normed.reshape(-1, model_width), w_in, preferred_element_type=jnp...]
    all_to_all x2 -> x0, waiting for transfers between devices: 13.3 us -> none  [the longest x1 13.3 us: shards(): lax.all_to_all(outgoing.reshape(peer_count, pair_depth * BLK, model_width...]
    all_to_all x2 -> x0, starting transfers between devices: 8.73 us -> none  [the longest x1 5.17 us: shards(): lax.all_to_all(outgoing.reshape(peer_count, pair_depth * BLK, model_width...]
    unnamed x17 -> x11, local copies, waits for them, and re-layouts: 1.41 us -> 6.56 us
    gather x8 -> x0, local copies, waits for them, and re-layouts: 4.78 us -> none  [the longest x2 0.86 us: shards(): picked = block_of[own_peer][jnp.minimum(offset, blocks - 1)]]
    select_n x9 -> x0, other arithmetic: 4.09 us -> none  [the longest x1 1.12 us: shards(): jnp.where(back_valid[:, :, None, None], grad_work[back_slot], jnp.zeros((...]
  transfers between devices with their start and end apart: 4 -> 0, of which waited for: 3 -> 0; matrix products, arithmetic and copies ran while one was open for 14% -> 0% of each run, Pallas kernels for 0% -> 0%
where the time goes in v1:
time: 54.1 us; the launch traced here: 53.8 us
  Pallas kernels  46.6 us (86%)
  local copies, waits for them, and re-layouts  6.56 us (12%)
  between operations  0.65 us (1%)
    pallas_call x1, Pallas kernels, fused_shards(): pl.pallas_call(functools.partial(fused, peers, groups), out_shape=(jax.Sh...  46.6 us
    unnamed x11, local copies, waits for them, and re-layouts  6.56 us

profile of v1, /device:TPU:0, one launch (start us, length us, event | category | flops | bytes accessed | tf_op | source)
XLA Modules:
  0.0 53.8 jit_solution(15260507559586293702)
XLA Ops:
  0.6 0.0 copy-start
  0.6 1.2 %copy-done = bf16[512,1024]{1,0:T(8,128)(2,1)S(1)} copy-done((bf16[512,1024]{1,0:T(8,128)(2,1)S(1)}, bf16[512,1024]{1,0:T(8,128)(2,1)}, u32[]{:S(2)}) %copy-start) | copy-done | bytes 1048600
  1.9 0.0 copy-start.1
  1.9 1.2 %copy-done.1 = bf16[512,1024]{1,0:T(8,128)(2,1)S(1)} copy-done((bf16[512,1024]{1,0:T(8,128)(2,1)S(1)}, bf16[512,1024]{1,0:T(8,128)(2,1)}, u32[]{:S(2)}) %copy-start.1) | copy-done | bytes 1048600
  3.1 0.0 copy-start.2
  3.1 1.0 %copy-done.2 = bf16[256,1024]{1,0:T(8,128)(2,1)S(1)} copy-done((bf16[256,1024]{1,0:T(8,128)(2,1)S(1)}, bf16[256,1024]{1,0:T(8,128)(2,1)}, u32[]{:S(2)}) %copy-start.2) | copy-done | bytes 524312
  4.1 0.0 copy-start.3
  4.1 0.7 %copy-done.3 = s32[1,512]{1,0:T(1,128)S(1)} copy-done((s32[1,512]{1,0:T(1,128)S(1)}, s32[1,512]{1,0:T(1,128)}, u32[]{:S(2)}) %copy-start.3) | copy-done | bytes 2072
  4.8 46.6 %shard_map.76 = (bf16[256,1024]{1,0:T(8,128)(2,1)S(1)}, bf16[512,1024]{1,0:T(8,128)(2,1)S(1)}, f32[64,256]{1,0:T(8,128)S(1)}) custom-call(s32[1,512]{1,0:T(1,128)S(1)} %copy-done.3, bf16[512,1024]{1,0:T(8,128)(2,1)S(1)} %copy-done, bf16[1024,2048]{1,0:T(8,128)(2,1)} %w_in_hbm.1, bf16[512,1024]{1,0:T(8,128)(2,1)S(1)} %copy-done.1, bf16[256,1024]{1,0:T(8,128)(2,1)S(1)} %copy-done.2), custom_call_target="tpu_custom_call" | custom-call | flops 5905580032 | bytes 8388608 | tf_op jit(solution)/shard_map/pallas_call | solution.py:691
  51.4 0.8 %copy.11 = bf16[256,1024]{1,0:T(8,128)(2,1)} copy(bf16[256,1024]{1,0:T(8,128)(2,1)S(1)} %get-tuple-element.6) | data formatting | bytes 1048576
  52.2 1.0 %copy.12 = bf16[512,1024]{1,0:T(8,128)(2,1)} copy(bf16[512,1024]{1,0:T(8,128)(2,1)S(1)} %get-tuple-element.7) | data formatting | bytes 2097152
  53.2 0.6 %copy.13 = f32[64,256]{1,0:T(8,128)} copy(f32[64,256]{1,0:T(8,128)S(1)} %get-tuple-element.8) | data formatting | bytes 131072
Async XLA Ops:
  0.6 1.2 %copy-start = (bf16[512,1024]{1,0:T(8,128)(2,1)S(1)}, bf16[512,1024]{1,0:T(8,128)(2,1)}, u32[]{:S(2)}) copy-start(bf16[512,1024]{1,0:T(8,128)(2,1)} %embed_hbm.1) | copy-start | bytes 3145732
  1.9 1.2 %copy-start.1 = (bf16[512,1024]{1,0:T(8,128)(2,1)S(1)}, bf16[512,1024]{1,0:T(8,128)(2,1)}, u32[]{:S(2)}) copy-start(bf16[512,1024]{1,0:T(8,128)(2,1)} %w_out_hbm.1) | copy-start | bytes 3145732
  3.1 1.0 %copy-start.2 = (bf16[256,1024]{1,0:T(8,128)(2,1)S(1)}, bf16[256,1024]{1,0:T(8,128)(2,1)}, u32[]{:S(2)}) copy-start(bf16[256,1024]{1,0:T(8,128)(2,1)} %cot_hbm.1) | copy-start | bytes 1572868
  4.1 0.7 %copy-start.3 = (s32[1,512]{1,0:T(1,128)S(1)}, s32[1,512]{1,0:T(1,128)}, u32[]{:S(2)}) copy-start(s32[1,512]{1,0:T(1,128)} %len_ref.1) | copy-start | bytes 6148

commit v2 on v1

--- a/solution.py
+++ b/solution.py
@@ -194,7 +194,7 @@
 def fused(
     peers,
     groups,
-    len_ref,
+    len_hbm,
     embed_hbm,
     w_in_hbm,
     w_out_hbm,
@@ -202,6 +202,7 @@
     out_ref,
     grad_ref,
     gproj_ref,
+    len_ref,
     cot_v,
     embed_v,
     w_in_v,
@@ -212,6 +213,9 @@
     orecv,
     take_ref,
     pack_ref,
+    unpack_ref,
+    untake_ref,
+    gated_t_ref,
     x_ref,
     nrm_ref,
     inv_ref,
@@ -256,7 +260,7 @@
     chunk = rows // peers
     blocks = rows // BLK
     total = len_ref.shape[1]
-    tile = min(rows, 256)
+    tile = rows
     tiles = rows // tile
     per_tile = tile // chunk
     bit_count = peers.bit_length() - 1
@@ -265,6 +269,21 @@
     gcols = width // groups
     half = peers // 2
 
+    len_load = pltpu.make_async_copy(len_hbm, len_ref, in_sem.at[4])
+    len_load.start()
+    loads = []
+    for place, (src, dst) in enumerate(
+        (
+            (cot_hbm, cot_v),
+            (embed_hbm, embed_v),
+            (w_in_hbm, w_in_v),
+            (w_out_hbm, w_out_v),
+        )
+    ):
+        load = pltpu.make_async_copy(src, dst, in_sem.at[place])
+        load.start()
+        loads.append(load)
+
     barrier = pltpu.get_barrier_semaphore()
     for j in range(1, peers):
         pl.semaphore_signal(
@@ -275,14 +294,7 @@
             barrier, inc=1, device_id={"group": lax.rem(grp + d, groups)}, device_id_type=MESH
         )
 
-    loads = []
-    for place, (src, dst) in enumerate(
-        ((cot_hbm, cot_v), (embed_hbm, embed_v), (w_in_hbm, w_in_v), (w_out_hbm, w_out_v))
-    ):
-        load = pltpu.make_async_copy(src, dst, in_sem.at[place])
-        load.start()
-        loads.append(load)
-
+    len_load.wait()
     lens = len_ref[...]
     live = jnp.where(lens > 0, 1.0, 0.0).astype(F32)
     lane = lax.broadcasted_iota(jnp.int32, (1, total), 1)
@@ -319,7 +331,7 @@
         csend[:, cols] = dotf(pack_ref[...], cot_v[:, cols]).astype(BF16)
         return 0
 
-    lax.fori_loop(0, width // col, pack, 0)
+    lax.fori_loop(0, width // col, pack, 0, unroll=True)
     pl.semaphore_wait(barrier, peers - 1 + groups - 1)
 
     def exchange(src, dst, s_sem, r_sem, j):
@@ -365,8 +377,15 @@
     row_in = lax.broadcasted_iota(jnp.int32, (rows, 1), 0) & (BLK - 1)
     valid_ref[...] = jnp.where(row_in.astype(F32) < slot_len, 1.0, 0.0)
 
+    def upright(line):
+        return jnp.transpose(jnp.broadcast_to(line.astype(F32), (128, line.shape[1])))[:, 0:1]
+
+    slots = lax.broadcasted_iota(jnp.int32, (1, rows), 1).astype(F32)
+    untake_ref[...] = jnp.where(upright(target) == slots, 1.0, 0.0).astype(BF16)
+    unpack_ref[...] = jnp.where(upright(wtarget) == slots, 1.0, 0.0).astype(BF16)
+
     out_moves = {j: exchange(osend, orecv, os_sem, or_sem, j) for j in range(1, peers)}
-    small = 32
+    small = 64
     scale = HD ** (-0.5)
     sub = min(tile, 128)
     si = lax.broadcasted_iota(jnp.int32, (sub, sub), 0)
@@ -383,7 +402,7 @@
             x_ref[span, cols] = dotf(take_ref[span, :], embed_v[:, cols]).astype(BF16)
             return 0
 
-        lax.fori_loop(0, width // col, pick, 0)
+        lax.fori_loop(0, width // col, pick, 0, unroll=True)
 
         def norm(s, _):
             part_rows = pl.ds(pl.multiple_of(t * tile + s * small, small), small)
@@ -394,7 +413,7 @@
             inv_ref[part_rows, :] = inv
             return 0
 
-        lax.fori_loop(0, tile // small, norm, 0)
+        lax.fori_loop(0, tile // small, norm, 0, unroll=4)
         if place == 0:
             loads[2].wait()
 
@@ -407,7 +426,7 @@
             der_ref[span, cols] = (sig + act * (1.0 - sig)).astype(BF16)
             return 0
 
-        lax.fori_loop(0, 4 * attn // col, project, 0)
+        lax.fori_loop(0, 4 * attn // col, project, 0, unroll=4)
 
         def attend(s, _):
             sr = pl.ds(pl.multiple_of(t * tile + s * sub, sub), sub)
@@ -436,10 +455,12 @@
                 var > MIX_FLOOR, 1.0, jnp.where(var == MIX_FLOOR, 0.5, 0.0)
             )
             y_ref[sr, :] = y.astype(BF16)
-            gated_ref[sr, :] = (y * act_ref[sr, pl.ds(0, attn)].astype(F32)).astype(BF16)
+            gated = y * act_ref[sr, pl.ds(0, attn)].astype(F32)
+            gated_ref[sr, :] = gated.astype(BF16)
+            gated_t_ref[:, sr] = jnp.transpose(gated).astype(BF16)
             return 0
 
-        lax.fori_loop(0, tile // sub, attend, 0)
+        lax.fori_loop(0, tile // sub, attend, 0, unroll=2)
         if place == 0:
             loads[3].wait()
 
@@ -449,7 +470,7 @@
             osend[span, cols] = jnp.where(valid_ref[span, :] > 0.0, out, 0.0).astype(BF16)
             return 0
 
-        lax.fori_loop(0, width // col, produce, 0)
+        lax.fori_loop(0, width // col, produce, 0, unroll=True)
         for j in reversed(range(t * per_tile, (t + 1) * per_tile)):
             if j:
                 out_moves[j].start()
@@ -464,14 +485,14 @@
         crecv[sr, :] = jnp.where(valid_ref[sr, :] > 0.0, got, 0.0).astype(BF16)
         return 0
 
-    lax.fori_loop(0, rows // small, mask, 0)
+    lax.fori_loop(0, rows // small, mask, 0, unroll=True)
 
     def outer(n, _):
         cols = pl.ds(pl.multiple_of(n * col, col), col)
-        gfull_ref[:, cols] = dotf(gated_ref[...], crecv[:, cols], TN)
+        gfull_ref[:, cols] = dotf(gated_t_ref[...], crecv[:, cols])
         return 0
 
-    lax.fori_loop(0, width // col, outer, 0)
+    lax.fori_loop(0, width // col, outer, 0, unroll=True)
     for m in range(half):
         theirs = pl.multiple_of(toggled(me, 2 * m + 1) * part, part)
         core_send[pl.ds(m * part, part), :] = gfull_ref[pl.ds(theirs, part), :].astype(BF16)
@@ -485,16 +506,14 @@
     )
     core_move.start()
 
+    def back_out(n, _):
+        cols = pl.ds(pl.multiple_of(n * col, col), col)
+        dg_ref[:, cols] = dotf(crecv[...], w_out_v[cols, :], NT).astype(BF16)
+        return 0
+
+    lax.fori_loop(0, attn // col, back_out, 0, unroll=True)
+
     def backward(t):
-        span = pl.ds(t * tile, tile)
-
-        def back_out(n, _):
-            cols = pl.ds(pl.multiple_of(n * col, col), col)
-            dg_ref[:, cols] = dotf(crecv[span, :], w_out_v[cols, :], NT).astype(BF16)
-            return 0
-
-        lax.fori_loop(0, attn // col, back_out, 0)
-
         def back_attend(s, _):
             here = pl.ds(pl.multiple_of(s * sub, sub), sub)
             sr = pl.ds(pl.multiple_of(t * tile + s * sub, sub), sub)
@@ -522,14 +541,14 @@
                     dproj_ref[here, place_of] = (grad * der_ref[sr, place_of].astype(F32)).astype(BF16)
             return 0
 
-        lax.fori_loop(0, tile // sub, back_attend, 0)
+        lax.fori_loop(0, tile // sub, back_attend, 0, unroll=2)
 
         def back_in(n, _):
             cols = pl.ds(pl.multiple_of(n * col, col), col)
             dn_ref[:, cols] = dotf(dproj_ref[...], w_in_v[cols, :], NT).astype(BF16)
             return 0
 
-        lax.fori_loop(0, width // col, back_in, 0)
+        lax.fori_loop(0, width // col, back_in, 0, unroll=True)
 
         def back_norm(s, _):
             here = pl.ds(pl.multiple_of(s * small, small), small)
@@ -541,7 +560,7 @@
             gradp_ref[sr, :] = (crecv[sr, :].astype(F32) + dx).astype(BF16)
             return 0
 
-        lax.fori_loop(0, tile // small, back_norm, 0)
+        lax.fori_loop(0, tile // small, back_norm, 0, unroll=4)
 
     z_moves = [
         pltpu.make_async_remote_copy(
@@ -565,22 +584,20 @@
         )
         for m in range(1, half)
     ]
-    for t in range(tiles):
-        backward(t)
-        if t == 0:
-            core_move.wait_recv()
-            for d in range(groups):
-                theirs = pl.ds(pl.multiple_of(lax.rem(grp + d, groups) * gcols, gcols), gcols)
-                for m in range(half):
-                    ours = pl.multiple_of(toggled(me, 2 * m) * part, part)
-                    mr = pl.ds(m * part, part)
-                    pair = gfull_ref[pl.ds(ours, part), theirs] + core_recv[mr, theirs].astype(F32)
-                    if d:
-                        z_send[d - 1, mr, :] = pair.astype(BF16)
-                    else:
-                        held_ref[mr, :] = pair
-                if d:
-                    z_moves[d - 1].start()
+    core_move.wait_recv()
+    for d in reversed(range(groups)):
+        theirs = pl.ds(pl.multiple_of(lax.rem(grp + d, groups) * gcols, gcols), gcols)
+        for m in range(half):
+            ours = pl.multiple_of(toggled(me, 2 * m) * part, part)
+            mr = pl.ds(m * part, part)
+            pair = gfull_ref[pl.ds(ours, part), theirs] + core_recv[mr, theirs].astype(F32)
+            if d:
+                z_send[d - 1, mr, :] = pair.astype(BF16)
+            else:
+                held_ref[mr, :] = pair
+        if d:
+            z_moves[d - 1].start()
+    backward(0)
 
     for move in z_moves:
         move.wait_recv()
@@ -597,20 +614,20 @@
 
     def unpack_grad(n, _):
         cols = pl.ds(pl.multiple_of(n * col, col), col)
-        grad_ref[:, cols] = dotf(take_ref[...], gradp_ref[:, cols], TN).astype(BF16)
+        grad_ref[:, cols] = dotf(untake_ref[...], gradp_ref[:, cols]).astype(BF16)
         return 0
 
-    lax.fori_loop(0, width // col, unpack_grad, 0)
+    lax.fori_loop(0, width // col, unpack_grad, 0, unroll=True)
 
     for j in range(1, peers):
         out_moves[j].wait_recv()
 
     def unpack_out(n, _):
         cols = pl.ds(pl.multiple_of(n * col, col), col)
-        out_ref[:, cols] = dotf(pack_ref[...], orecv[:, cols], TN).astype(BF16)
+        out_ref[:, cols] = dotf(unpack_ref[...], orecv[:, cols]).astype(BF16)
         return 0
 
-    lax.fori_loop(0, width // col, unpack_out, 0)
+    lax.fori_loop(0, width // col, unpack_out, 0, unroll=True)
 
     share = held_ref[pl.ds(0, part), :]
     for m in range(1, half):
@@ -632,7 +649,7 @@
     rows, width = embed.shape
     work_rows = cotangent.shape[0]
     attn = w_out.shape[0]
-    tile = min(rows, 256)
+    tile = rows
     sub = min(tile, 128)
     heads = attn // HD
     part = attn // peers
@@ -641,6 +658,7 @@
     vmem = pltpu.VMEM
     dma = pltpu.SemaphoreType.DMA
     scratch = [
+        vmem(lengths.shape, jnp.int32),
         vmem((work_rows, width), BF16),
         vmem((rows, width), BF16),
         vmem(w_in.shape, BF16),
@@ -651,6 +669,9 @@
         vmem((rows, width), BF16),
         vmem((rows, rows), BF16),
         vmem((rows, work_rows), BF16),
+        vmem((work_rows, rows), BF16),
+        vmem((rows, rows), BF16),
+        vmem((attn, rows), BF16),
         vmem((rows, width), BF16),
         vmem((rows, width), BF16),
         vmem((rows, 1), F32),
@@ -675,7 +696,7 @@
         vmem((groups - 1, half * part, gcols), BF16),
         vmem((half - 1, part, gcols), BF16),
         vmem((half - 1, part, gcols), BF16),
-        dma((4,)),
+        dma((5,)),
         dma((peers,)),
         dma((peers,)),
         dma((peers,)),
@@ -686,7 +707,7 @@
         dma((half - 1,)),
         dma((half - 1,)),
     ]
-    anywhere = pl.BlockSpec(memory_space=pl.ANY)
+    pinned = pl.BlockSpec(memory_space=pltpu.HBM)
     resident = pl.BlockSpec(memory_space=pltpu.VMEM)
     return pl.pallas_call(
         functools.partial(fused, peers, groups),
@@ -695,11 +716,11 @@
             jax.ShapeDtypeStruct((rows, width), BF16),
             jax.ShapeDtypeStruct((part, gcols), F32),
         ),
-        in_specs=[resident] + [anywhere] * 4,
+        in_specs=[pinned] * 5,
         out_specs=(resident, resident, resident),
         scratch_shapes=scratch,
         compiler_params=pltpu.CompilerParams(
-            collective_id=0, has_side_effects=True, vmem_limit_bytes=48 * 1024 * 1024
+            collective_id=0, has_side_effects=True, vmem_limit_bytes=60 * 1024 * 1024
         ),
         cost_estimate=pl.CostEstimate(
             flops=2 * rows * width * attn * 11,

time: 54.1 us -> 46.8 us (0.87)
  Pallas kernels: 46.6 us -> 40.3 us
  local copies, waits for them, and re-layouts: 6.56 us -> 5.6 us
    pallas_call x1, Pallas kernels: 46.6 us -> 40.3 us  [fused_shards(): pl.pallas_call(functools.partial(fused, peers, groups), out_shape=(jax.Sh...]
    unnamed x11 -> x3, local copies, waits for them, and re-layouts: 6.56 us -> 5.6 us
where the time goes in v2:
time: 46.8 us; the launch traced here: 46.6 us
  Pallas kernels  40.3 us (86%)
  local copies, waits for them, and re-layouts  5.6 us (12%)
  between operations  0.64 us (1%)
    pallas_call x1, Pallas kernels, fused_shards(): pl.pallas_call(functools.partial(fused, peers, groups), out_shape=(jax.Sh...  40.3 us
    unnamed x3, local copies, waits for them, and re-layouts  5.6 us

profile of v2, /device:TPU:0, one launch (start us, length us, event | category | flops | bytes accessed | tf_op | source)
XLA Modules:
  0.0 46.6 jit_solution(8365157950030257380)
XLA Ops:
  0.6 40.3 %shard_map.76 = (bf16[256,1024]{1,0:T(8,128)(2,1)}, bf16[512,1024]{1,0:T(8,128)(2,1)}, f32[64,256]{1,0:T(8,128)}) custom-call(s32[1,512]{1,0:T(1,128)} %len_hbm.1, bf16[512,1024]{1,0:T(8,128)(2,1)} %embed_hbm.1, bf16[1024,2048]{1,0:T(8,128)(2,1)} %w_in_hbm.1, bf16[512,1024]{1,0:T(8,128)(2,1)} %w_out_hbm.1, bf16[256,1024]{1,0:T(8,128)(2,1)} %cot_hbm.1), custom_call_target="tpu_custom_call" | custom-call | flops 5905580032 | bytes 8388608 | tf_op jit(solution)/shard_map/pallas_call | solution.py:712
  40.9 1.9 %copy.11 = bf16[256,1024]{1,0:T(8,128)(2,1)} copy(bf16[256,1024]{1,0:T(8,128)(2,1)} %get-tuple-element.6) | data formatting | bytes 1048576
  42.8 2.3 %copy.12 = bf16[512,1024]{1,0:T(8,128)(2,1)} copy(bf16[512,1024]{1,0:T(8,128)(2,1)} %get-tuple-element.7) | data formatting | bytes 2097152
  45.1 1.5 %copy.13 = f32[64,256]{1,0:T(8,128)} copy(f32[64,256]{1,0:T(8,128)} %get-tuple-element.8) | data formatting | bytes 131072

commit v3 on v2

--- a/solution.py
+++ b/solution.py
@@ -236,10 +236,15 @@
     core_send,
     core_recv,
     held_ref,
+    kept_ref,
     z_send,
     z_recv,
     p_send,
     p_recv,
+    q_send,
+    q_recv,
+    r_send,
+    r_recv,
     in_sem,
     cs_sem,
     cr_sem,
@@ -250,6 +255,10 @@
     zr_sem,
     ps_sem,
     pr_sem,
+    qs_sem,
+    qr_sem,
+    rs_sem,
+    rr_sem,
 ):
     me = lax.axis_index("peer")
     grp = lax.axis_index("group")
@@ -262,12 +271,13 @@
     total = len_ref.shape[1]
     tile = rows
     tiles = rows // tile
-    per_tile = tile // chunk
     bit_count = peers.bit_length() - 1
     col = 256
     part = attn // peers
     gcols = width // groups
     half = peers // 2
+    zpart = part // 2
+    qpart = part - zpart
 
     len_load = pltpu.make_async_copy(len_hbm, len_ref, in_sem.at[4])
     len_load.start()
@@ -326,14 +336,6 @@
 
     loads[0].wait()
 
-    def pack(n, _):
-        cols = pl.ds(pl.multiple_of(n * col, col), col)
-        csend[:, cols] = dotf(pack_ref[...], cot_v[:, cols]).astype(BF16)
-        return 0
-
-    lax.fori_loop(0, width // col, pack, 0, unroll=True)
-    pl.semaphore_wait(barrier, peers - 1 + groups - 1)
-
     def exchange(src, dst, s_sem, r_sem, j):
         span = pl.ds(j * chunk, chunk)
         return pltpu.make_async_remote_copy(
@@ -346,8 +348,14 @@
         )
 
     cot_moves = {j: exchange(csend, crecv, cs_sem, cr_sem, j) for j in range(1, peers)}
-    for j in reversed(range(1, peers)):
-        cot_moves[j].start()
+    for u in reversed(range(half)):
+        duo = pl.ds(u * 2 * chunk, 2 * chunk)
+        csend[duo, :] = dotf(pack_ref[duo, :], cot_v[...]).astype(BF16)
+        if u == half - 1:
+            pl.semaphore_wait(barrier, peers - 1 + groups - 1)
+        for j in (2 * u + 1, 2 * u):
+            if j:
+                cot_moves[j].start()
     crecv[pl.ds(0, chunk), :] = csend[pl.ds(0, chunk), :]
 
     spot = lax.broadcasted_iota(jnp.int32, (16, total), 0)
@@ -471,13 +479,12 @@
             return 0
 
         lax.fori_loop(0, width // col, produce, 0, unroll=True)
-        for j in reversed(range(t * per_tile, (t + 1) * per_tile)):
-            if j:
-                out_moves[j].start()
     orecv[pl.ds(0, chunk), :] = osend[pl.ds(0, chunk), :]
 
     for j in range(1, peers):
         cot_moves[j].wait_recv()
+    for j in reversed(range(1, peers)):
+        out_moves[j].start()
 
     def mask(s, _):
         sr = pl.ds(pl.multiple_of(s * small, small), small)
@@ -550,6 +557,33 @@
 
         lax.fori_loop(0, width // col, back_in, 0, unroll=True)
 
+        for move in q_moves:
+            move.wait_recv()
+        mine = pl.ds(pl.multiple_of(grp * gcols, gcols), gcols)
+        for d in reversed(range(groups)):
+            theirs = pl.ds(pl.multiple_of(lax.rem(grp + d, groups) * gcols, gcols), gcols)
+            share = kept_ref[:, theirs]
+            for m in range(1, half):
+                share = share + q_recv[m - 1, :, theirs].astype(F32)
+            if d:
+                r_send[d - 1] = share.astype(BF16)
+                r_moves[d - 1].start()
+            else:
+                kept_ref[:, mine] = share
+
+        for move in z_moves:
+            move.wait_recv()
+        for m in reversed(range(half)):
+            mr = pl.ds(m * zpart, zpart)
+            share = held_ref[mr, :]
+            for d in range(1, groups):
+                share = share + z_recv[d - 1, mr, :].astype(F32)
+            if m:
+                p_send[m - 1] = share.astype(BF16)
+                p_moves[m - 1].start()
+            else:
+                held_ref[mr, :] = share
+
         def back_norm(s, _):
             here = pl.ds(pl.multiple_of(s * small, small), small)
             sr = pl.ds(pl.multiple_of(t * tile + s * small, small), small)
@@ -573,6 +607,28 @@
         )
         for d in range(1, groups)
     ]
+    r_moves = [
+        pltpu.make_async_remote_copy(
+            src_ref=r_send.at[d - 1],
+            dst_ref=r_recv.at[d - 1],
+            send_sem=rs_sem.at[d - 1],
+            recv_sem=rr_sem.at[d - 1],
+            device_id={"group": lax.rem(grp + d, groups)},
+            device_id_type=MESH,
+        )
+        for d in range(1, groups)
+    ]
+    q_moves = [
+        pltpu.make_async_remote_copy(
+            src_ref=q_send.at[m - 1],
+            dst_ref=q_recv.at[m - 1],
+            send_sem=qs_sem.at[m - 1],
+            recv_sem=qr_sem.at[m - 1],
+            device_id={"peer": toggled(me, 2 * m)},
+            device_id_type=MESH,
+        )
+        for m in range(1, half)
+    ]
     p_moves = [
         pltpu.make_async_remote_copy(
             src_ref=p_send.at[m - 1],
@@ -589,28 +645,25 @@
         theirs = pl.ds(pl.multiple_of(lax.rem(grp + d, groups) * gcols, gcols), gcols)
         for m in range(half):
             ours = pl.multiple_of(toggled(me, 2 * m) * part, part)
-            mr = pl.ds(m * part, part)
-            pair = gfull_ref[pl.ds(ours, part), theirs] + core_recv[mr, theirs].astype(F32)
+            pair = gfull_ref[pl.ds(ours, zpart), theirs]
+            pair = pair + core_recv[pl.ds(m * part, zpart), theirs].astype(F32)
+            mr = pl.ds(m * zpart, zpart)
             if d:
                 z_send[d - 1, mr, :] = pair.astype(BF16)
             else:
                 held_ref[mr, :] = pair
         if d:
             z_moves[d - 1].start()
+    for m in reversed(range(half)):
+        ours = pl.multiple_of(toggled(me, 2 * m) * part + zpart, qpart)
+        pair = gfull_ref[pl.ds(ours, qpart), :]
+        pair = pair + core_recv[pl.ds(m * part + zpart, qpart), :].astype(F32)
+        if m:
+            q_send[m - 1] = pair.astype(BF16)
+            q_moves[m - 1].start()
+        else:
+            kept_ref[...] = pair
     backward(0)
-
-    for move in z_moves:
-        move.wait_recv()
-    for m in reversed(range(half)):
-        mr = pl.ds(m * part, part)
-        share = held_ref[mr, :]
-        for d in range(1, groups):
-            share = share + z_recv[d - 1, mr, :].astype(F32)
-        if m:
-            p_send[m - 1] = share.astype(BF16)
-            p_moves[m - 1].start()
-        else:
-            held_ref[mr, :] = share
 
     def unpack_grad(n, _):
         cols = pl.ds(pl.multiple_of(n * col, col), col)
@@ -629,17 +682,23 @@
 
     lax.fori_loop(0, width // col, unpack_out, 0, unroll=True)
 
-    share = held_ref[pl.ds(0, part), :]
+    grad_scale = 1.0 / math.sqrt(groups * peers * work_rows)
+    share = held_ref[pl.ds(0, zpart), :]
     for m in range(1, half):
         p_moves[m - 1].wait_recv()
         share = share + p_recv[m - 1].astype(F32)
-    gproj_ref[...] = share * (1.0 / math.sqrt(groups * peers * work_rows))
+    gproj_ref[pl.ds(0, zpart), :] = share * grad_scale
+    share = kept_ref[:, pl.ds(pl.multiple_of(grp * gcols, gcols), gcols)]
+    for d in range(1, groups):
+        r_moves[d - 1].wait_recv()
+        share = share + r_recv[d - 1].astype(F32)
+    gproj_ref[pl.ds(zpart, qpart), :] = share * grad_scale
 
     for j in range(1, peers):
         cot_moves[j].wait_send()
         out_moves[j].wait_send()
     core_move.wait_send()
-    for move in z_moves + p_moves:
+    for move in z_moves + p_moves + q_moves + r_moves:
         move.wait_send()
 
 
@@ -691,11 +750,16 @@
         vmem((attn, width), F32),
         vmem((half * part, width), BF16),
         vmem((half * part, width), BF16),
-        vmem((half * part, gcols), F32),
-        vmem((groups - 1, half * part, gcols), BF16),
-        vmem((groups - 1, half * part, gcols), BF16),
-        vmem((half - 1, part, gcols), BF16),
-        vmem((half - 1, part, gcols), BF16),
+        vmem((half * (part // 2), gcols), F32),
+        vmem((part - part // 2, width), F32),
+        vmem((groups - 1, half * (part // 2), gcols), BF16),
+        vmem((groups - 1, half * (part // 2), gcols), BF16),
+        vmem((half - 1, part // 2, gcols), BF16),
+        vmem((half - 1, part // 2, gcols), BF16),
+        vmem((half - 1, part - part // 2, width), BF16),
+        vmem((half - 1, part - part // 2, width), BF16),
+        vmem((groups - 1, part - part // 2, gcols), BF16),
+        vmem((groups - 1, part - part // 2, gcols), BF16),
         dma((5,)),
         dma((peers,)),
         dma((peers,)),
@@ -706,6 +770,10 @@
         dma((groups - 1,)),
         dma((half - 1,)),
         dma((half - 1,)),
+        dma((half - 1,)),
+        dma((half - 1,)),
+        dma((groups - 1,)),
+        dma((groups - 1,)),
     ]
     pinned = pl.BlockSpec(memory_space=pltpu.HBM)
     resident = pl.BlockSpec(memory_space=pltpu.VMEM)
@@ -720,7 +788,7 @@
         out_specs=(resident, resident, resident),
         scratch_shapes=scratch,
         compiler_params=pltpu.CompilerParams(
-            collective_id=0, has_side_effects=True, vmem_limit_bytes=60 * 1024 * 1024
+            collective_id=0, has_side_effects=True, vmem_limit_bytes=54_000_000
         ),
         cost_estimate=pl.CostEstimate(
             flops=2 * rows * width * attn * 11,
@@ -744,7 +812,7 @@
             and rows % 256 == 0
             and 256 % (rows // peers) == 0
             and left == 0
-            and part % 16 == 0
+            and part % 32 == 0
             and embed.shape[1] % (256 * mesh.shape["group"]) == 0
             and lengths.shape[1] * BLK == rows * peers
         )

time: 46.8 us -> 44.2 us (0.944)
  local copies, waits for them, and re-layouts: 5.6 us -> 4.11 us
  Pallas kernels: 40.3 us -> 39.3 us
    unnamed x3 -> x7, local copies, waits for them, and re-layouts: 5.6 us -> 4.11 us
    pallas_call x1, Pallas kernels: 40.3 us -> 39.3 us  [fused_shards(): pl.pallas_call(functools.partial(fused, peers, groups), out_shape=(jax.Sh...]
where the time goes in v3:
time: 44.2 us; the launch traced here: 44 us
  Pallas kernels  39.3 us (89%)
  local copies, waits for them, and re-layouts  4.11 us (9%)
  between operations  0.65 us (1%)
    pallas_call x1, Pallas kernels, fused_shards(): pl.pallas_call(functools.partial(fused, peers, groups), out_shape=(jax.Sh...  39.3 us
    unnamed x7, local copies, waits for them, and re-layouts  4.11 us

profile of v3, /device:TPU:0, one launch (start us, length us, event | category | flops | bytes accessed | tf_op | source)
XLA Modules:
  0.0 44.0 jit_solution(13974942261476021955)
XLA Ops:
  0.6 0.0 copy-start
  0.6 1.0 %copy-done = bf16[256,1024]{1,0:T(8,128)(2,1)S(1)} copy-done((bf16[256,1024]{1,0:T(8,128)(2,1)S(1)}, bf16[256,1024]{1,0:T(8,128)(2,1)}, u32[]{:S(2)}) %copy-start) | copy-done | bytes 524312
  1.7 0.0 copy-start.1
  1.7 0.7 %copy-done.1 = s32[1,512]{1,0:T(1,128)S(1)} copy-done((s32[1,512]{1,0:T(1,128)S(1)}, s32[1,512]{1,0:T(1,128)}, u32[]{:S(2)}) %copy-start.1) | copy-done | bytes 2072
  2.4 39.3 %shard_map.76 = (bf16[256,1024]{1,0:T(8,128)(2,1)S(1)}, bf16[512,1024]{1,0:T(8,128)(2,1)S(1)}, f32[64,256]{1,0:T(8,128)S(1)}) custom-call(s32[1,512]{1,0:T(1,128)S(1)} %copy-done.1, bf16[512,1024]{1,0:T(8,128)(2,1)} %embed_hbm.1, bf16[1024,2048]{1,0:T(8,128)(2,1)} %w_in_hbm.1, bf16[512,1024]{1,0:T(8,128)(2,1)} %w_out_hbm.1, bf16[256,1024]{1,0:T(8,128)(2,1)S(1)} %copy-done), custom_call_target="tpu_custom_call" | custom-call | flops 5905580032 | bytes 8388608 | tf_op jit(solution)/shard_map/pallas_call | solution.py:780
  41.7 0.8 %copy.11 = bf16[256,1024]{1,0:T(8,128)(2,1)} copy(bf16[256,1024]{1,0:T(8,128)(2,1)S(1)} %get-tuple-element.6) | data formatting | bytes 1048576
  42.4 1.0 %copy.12 = bf16[512,1024]{1,0:T(8,128)(2,1)} copy(bf16[512,1024]{1,0:T(8,128)(2,1)S(1)} %get-tuple-element.7) | data formatting | bytes 2097152
  43.4 0.6 %copy.13 = f32[64,256]{1,0:T(8,128)} copy(f32[64,256]{1,0:T(8,128)S(1)} %get-tuple-element.8) | data formatting | bytes 131072
Async XLA Ops:
  0.6 1.0 %copy-start = (bf16[256,1024]{1,0:T(8,128)(2,1)S(1)}, bf16[256,1024]{1,0:T(8,128)(2,1)}, u32[]{:S(2)}) copy-start(bf16[256,1024]{1,0:T(8,128)(2,1)} %cot_hbm.1) | copy-start | bytes 1572868
  1.7 0.7 %copy-start.1 = (s32[1,512]{1,0:T(1,128)S(1)}, s32[1,512]{1,0:T(1,128)}, u32[]{:S(2)}) copy-start(s32[1,512]{1,0:T(1,128)} %len_hbm.1) | copy-start | bytes 6148

commit v4 on v3

--- a/solution.py
+++ b/solution.py
@@ -269,7 +269,7 @@
     chunk = rows // peers
     blocks = rows // BLK
     total = len_ref.shape[1]
-    tile = rows
+    tile = min(rows, 256)
     tiles = rows // tile
     bit_count = peers.bit_length() - 1
     col = 256
@@ -421,7 +421,7 @@
             inv_ref[part_rows, :] = inv
             return 0
 
-        lax.fori_loop(0, tile // small, norm, 0, unroll=4)
+        lax.fori_loop(0, tile // small, norm, 0, unroll=True)
         if place == 0:
             loads[2].wait()
 
@@ -434,7 +434,7 @@
             der_ref[span, cols] = (sig + act * (1.0 - sig)).astype(BF16)
             return 0
 
-        lax.fori_loop(0, 4 * attn // col, project, 0, unroll=4)
+        lax.fori_loop(0, 4 * attn // col, project, 0, unroll=True)
 
         def attend(s, _):
             sr = pl.ds(pl.multiple_of(t * tile + s * sub, sub), sub)
@@ -468,7 +468,7 @@
             gated_t_ref[:, sr] = jnp.transpose(gated).astype(BF16)
             return 0
 
-        lax.fori_loop(0, tile // sub, attend, 0, unroll=2)
+        lax.fori_loop(0, tile // sub, attend, 0, unroll=True)
         if place == 0:
             loads[3].wait()
 
@@ -479,20 +479,13 @@
             return 0
 
         lax.fori_loop(0, width // col, produce, 0, unroll=True)
+        for j in reversed(range(t * tile // chunk, (t + 1) * tile // chunk)):
+            if j:
+                out_moves[j].start()
     orecv[pl.ds(0, chunk), :] = osend[pl.ds(0, chunk), :]
 
     for j in range(1, peers):
         cot_moves[j].wait_recv()
-    for j in reversed(range(1, peers)):
-        out_moves[j].start()
-
-    def mask(s, _):
-        sr = pl.ds(pl.multiple_of(s * small, small), small)
-        got = crecv[sr, :].astype(F32)
-        crecv[sr, :] = jnp.where(valid_ref[sr, :] > 0.0, got, 0.0).astype(BF16)
-        return 0
-
-    lax.fori_loop(0, rows // small, mask, 0, unroll=True)
 
     def outer(n, _):
         cols = pl.ds(pl.multiple_of(n * col, col), col)
@@ -520,11 +513,11 @@
 
     lax.fori_loop(0, attn // col, back_out, 0, unroll=True)
 
-    def backward(t):
+    def backward():
         def back_attend(s, _):
             here = pl.ds(pl.multiple_of(s * sub, sub), sub)
-            sr = pl.ds(pl.multiple_of(t * tile + s * sub, sub), sub)
-            dg = dg_ref[here, :].astype(F32)
+            sr = pl.ds(pl.multiple_of(s * sub, sub), sub)
+            dg = dg_ref[here, :].astype(F32) * valid_ref[sr, :]
             y = y_ref[sr, :].astype(F32)
             gate = pl.ds(0, attn)
             dgate = (dg * y).astype(BF16).astype(F32)
@@ -548,7 +541,7 @@
                     dproj_ref[here, place_of] = (grad * der_ref[sr, place_of].astype(F32)).astype(BF16)
             return 0
 
-        lax.fori_loop(0, tile // sub, back_attend, 0, unroll=2)
+        lax.fori_loop(0, rows // sub, back_attend, 0, unroll=True)
 
         def back_in(n, _):
             cols = pl.ds(pl.multiple_of(n * col, col), col)
@@ -586,15 +579,15 @@
 
         def back_norm(s, _):
             here = pl.ds(pl.multiple_of(s * small, small), small)
-            sr = pl.ds(pl.multiple_of(t * tile + s * small, small), small)
+            sr = pl.ds(pl.multiple_of(s * small, small), small)
             dn = dn_ref[here, :].astype(F32)
             xh = nrm_ref[sr, :].astype(F32)
             dc = (dn - xh * jnp.mean(dn * xh, axis=1, keepdims=True)) * inv_ref[sr, :]
             dx = dc - jnp.mean(dc, axis=1, keepdims=True)
-            gradp_ref[sr, :] = (crecv[sr, :].astype(F32) + dx).astype(BF16)
+            gradp_ref[sr, :] = (crecv[sr, :].astype(F32) * valid_ref[sr, :] + dx).astype(BF16)
             return 0
 
-        lax.fori_loop(0, tile // small, back_norm, 0, unroll=4)
+        lax.fori_loop(0, rows // small, back_norm, 0, unroll=True)
 
     z_moves = [
         pltpu.make_async_remote_copy(
@@ -663,7 +656,7 @@
             q_moves[m - 1].start()
         else:
             kept_ref[...] = pair
-    backward(0)
+    backward()
 
     def unpack_grad(n, _):
         cols = pl.ds(pl.multiple_of(n * col, col), col)

time: 44.2 us -> 42.1 us (0.952)
  Pallas kernels: 39.3 us -> 37.2 us
    pallas_call x1, Pallas kernels: 39.3 us -> 37.2 us  [fused_shards(): pl.pallas_call(functools.partial(fused, peers, groups), out_shape=(jax.Sh...]
where the time goes in v4:
time: 42.1 us; the launch traced here: 41.9 us
  Pallas kernels  37.2 us (88%)
  local copies, waits for them, and re-layouts  4.11 us (10%)
  between operations  0.65 us (2%)
    pallas_call x1, Pallas kernels, fused_shards(): pl.pallas_call(functools.partial(fused, peers, groups), out_shape=(jax.Sh...  37.2 us
    unnamed x7, local copies, waits for them, and re-layouts  4.11 us

profile of v4, /device:TPU:0, one launch (start us, length us, event | category | flops | bytes accessed | tf_op | source)
XLA Modules:
  0.0 41.9 jit_solution(14926330752021827906)
XLA Ops:
  0.6 0.0 copy-start
  0.6 1.0 %copy-done = bf16[256,1024]{1,0:T(8,128)(2,1)S(1)} copy-done((bf16[256,1024]{1,0:T(8,128)(2,1)S(1)}, bf16[256,1024]{1,0:T(8,128)(2,1)}, u32[]{:S(2)}) %copy-start) | copy-done | bytes 524312
  1.7 0.0 copy-start.1
  1.7 0.7 %copy-done.1 = s32[1,512]{1,0:T(1,128)S(1)} copy-done((s32[1,512]{1,0:T(1,128)S(1)}, s32[1,512]{1,0:T(1,128)}, u32[]{:S(2)}) %copy-start.1) | copy-done | bytes 2072
  2.4 37.2 %shard_map.76 = (bf16[256,1024]{1,0:T(8,128)(2,1)S(1)}, bf16[512,1024]{1,0:T(8,128)(2,1)S(1)}, f32[64,256]{1,0:T(8,128)S(1)}) custom-call(s32[1,512]{1,0:T(1,128)S(1)} %copy-done.1, bf16[512,1024]{1,0:T(8,128)(2,1)} %embed_hbm.1, bf16[1024,2048]{1,0:T(8,128)(2,1)} %w_in_hbm.1, bf16[512,1024]{1,0:T(8,128)(2,1)} %w_out_hbm.1, bf16[256,1024]{1,0:T(8,128)(2,1)S(1)} %copy-done), custom_call_target="tpu_custom_call" | custom-call | flops 5905580032 | bytes 8388608 | tf_op jit(solution)/shard_map/pallas_call | solution.py:773
  39.6 0.8 %copy.11 = bf16[256,1024]{1,0:T(8,128)(2,1)} copy(bf16[256,1024]{1,0:T(8,128)(2,1)S(1)} %get-tuple-element.6) | data formatting | bytes 1048576
  40.3 1.0 %copy.12 = bf16[512,1024]{1,0:T(8,128)(2,1)} copy(bf16[512,1024]{1,0:T(8,128)(2,1)S(1)} %get-tuple-element.7) | data formatting | bytes 2097152
  41.3 0.6 %copy.13 = f32[64,256]{1,0:T(8,128)} copy(f32[64,256]{1,0:T(8,128)S(1)} %get-tuple-element.8) | data formatting | bytes 131072
Async XLA Ops:
  0.6 1.0 %copy-start = (bf16[256,1024]{1,0:T(8,128)(2,1)S(1)}, bf16[256,1024]{1,0:T(8,128)(2,1)}, u32[]{:S(2)}) copy-start(bf16[256,1024]{1,0:T(8,128)(2,1)} %cot_hbm.1) | copy-start | bytes 1572868
  1.7 0.7 %copy-start.1 = (s32[1,512]{1,0:T(1,128)S(1)}, s32[1,512]{1,0:T(1,128)}, u32[]{:S(2)}) copy-start(s32[1,512]{1,0:T(1,128)} %len_hbm.1) | copy-start | bytes 6148
